TPU v7x, 32 devices: a whole 2x2x4 slice. The times are simulated.
32 devices in a mesh: groups: 2 (over y), space: 4 (over z), date: 4 (over x, core).
Axes of the slice: x: 2, y: 2, z: 4, core: 2. Of those that a mesh axis runs over, the one named last changes fastest.
Arguments:
- features: bfloat16 [64, 256, 768], P('date', ('groups', 'space')), parts along dimension 1, may hold values from -6 to 6
- grad_out: bfloat16 [64, 256, 768], P('date', ('groups', 'space')), parts along dimension 1, may hold values from -6 to 6
- w_qkv: bfloat16 [768, 2304], replicated, may hold values from -2 to 2
- w_out: bfloat16 [768, 768], replicated, may hold values from -0.21875 to 0.21875
- valid_dates: int32 [64, 256], P(None, ('groups', 'space', 'date')), parts along dimension 1, may hold values 0 or 1
Outputs:
- grad_in: bfloat16 [64, 256, 768], P('date', ('groups', 'space')), parts along dimension 1
- weight_grad: float32 [1536, 3072], P(('groups', 'space', 'date')), parts along dimension 0
There are 2 independent parts, one for each index of `groups`. A program takes and returns all parts, laid end to end along the dimension named above; an argument that names none is the same for every part. Nothing has to cross between parts.
All inputs are finite; a program needn't handle non-finite values. No bound on the sum of `valid_dates` on one device may be relied on, other than what follows from the above.
Results may differ from a plain program's by a relative error of at most 0.009.
Values may be sent and summed in bfloat16 or wider, within the bound.
A program may use at most 128 MiB of HBM per device.

v0:
```python
import jax
import jax.numpy as jnp
from jax import lax
from jax.sharding import PartitionSpec as P

H = 12
HD = 64


epsilon = 1e-05


def normalize(features):
    flat = features.astype(jnp.float32)
    average = jnp.mean(flat, axis=-1, keepdims=True)
    centred = flat - average
    variance = jnp.mean(centred * centred, axis=-1, keepdims=True)
    inv_std = lax.rsqrt(variance + epsilon)
    return (centred * inv_std, inv_std)


def attend(qkv_all, d_attn_all, valid_dates):
    dates, patches, triple = qkv_all.shape
    width = triple // 3
    parted = qkv_all.reshape(dates, patches, 3, H, HD)
    query = parted[:, :, 0]
    keys = parted[:, :, 1]
    values = parted[:, :, 2]
    d_attn = d_attn_all.reshape(dates, patches, H, HD)
    scale = 1.0 / HD**0.5
    scores = jnp.einsum("tphd,uphd->phtu", query, keys, preferred_element_type=jnp.float32) * scale
    diagonal = jnp.arange(dates)[:, None] == jnp.arange(dates)[None, :]
    keep = (valid_dates.T[:, None, None, :] == 1) | diagonal[None, None]
    scores = jnp.where(keep, scores, -1e30)
    highest = jnp.max(scores, axis=-1, keepdims=True)
    expon = jnp.where(keep, jnp.exp(scores - highest), 0.0)
    prob = expon / jnp.sum(expon, axis=-1, keepdims=True)
    prob_b = prob.astype(jnp.bfloat16)
    attn = jnp.einsum("phtu,uphd->tphd", prob_b, values, preferred_element_type=jnp.float32).astype(
        jnp.bfloat16
    )
    d_prob = jnp.einsum("tphd,uphd->phtu", d_attn, values, preferred_element_type=jnp.float32)
    delta = jnp.sum(prob * d_prob, axis=-1, keepdims=True)
    d_score = (prob * (d_prob - delta) * scale).astype(jnp.bfloat16)
    d_query = jnp.einsum(
        "phtu,uphd->tphd", d_score, keys, preferred_element_type=jnp.float32
    ).astype(jnp.bfloat16)
    d_key = jnp.einsum(
        "phtu,tphd->uphd", d_score, query, preferred_element_type=jnp.float32
    ).astype(jnp.bfloat16)
    d_value = jnp.einsum(
        "phtu,tphd->uphd", prob_b, d_attn, preferred_element_type=jnp.float32
    ).astype(jnp.bfloat16)
    d_qkv = jnp.stack([d_query, d_key, d_value], axis=2).reshape(dates, patches, 3 * width)
    return (attn.reshape(dates, patches, width), d_qkv)


def norm_backward(grad_out, d_normed, normed, inv_std):
    first = jnp.mean(d_normed, axis=-1, keepdims=True)
    second = jnp.mean(d_normed * normed, axis=-1, keepdims=True)
    return (grad_out.astype(jnp.float32) + inv_std * (d_normed - first - normed * second)).astype(
        jnp.bfloat16
    )


def project_in(normed_b, w_qkv):
    dates, patches, width = normed_b.shape
    flat = jnp.dot(
        normed_b.reshape(dates * patches, width), w_qkv, preferred_element_type=jnp.float32
    )
    return flat.astype(jnp.bfloat16).reshape(dates, patches, 3 * width)


def project_grad(grad_out, w_out):
    dates, patches, width = grad_out.shape
    flat = lax.dot_general(
        grad_out.reshape(dates * patches, width),
        w_out,
        (((1,), (1,)), ((), ())),
        preferred_element_type=jnp.float32,
    )
    return flat.astype(jnp.bfloat16).reshape(dates, patches, width)


def back_normed(d_qkv, w_qkv):
    dates, patches, triple = d_qkv.shape
    flat = lax.dot_general(
        d_qkv.reshape(dates * patches, triple),
        w_qkv,
        (((1,), (1,)), ((), ())),
        preferred_element_type=jnp.float32,
    )
    return flat.reshape(dates, patches, triple // 3)


def local(features, grad_out, w_qkv, w_out, valid_dates):
    width = features.shape[-1]
    normed, inv_std = normalize(features)
    normed_b = normed.astype(jnp.bfloat16)
    qkv_local = project_in(normed_b, w_qkv)
    d_attn_local = project_grad(grad_out, w_out)
    qkv_all, d_attn_all = (
        lax.all_to_all(qkv_local, "date", split_axis=1, concat_axis=0, tiled=True),
        lax.all_to_all(d_attn_local, "date", split_axis=1, concat_axis=0, tiled=True),
    )
    attn_all, d_qkv_all = attend(qkv_all, d_attn_all, valid_dates)
    attn, d_qkv = (
        lax.all_to_all(attn_all, "date", split_axis=0, concat_axis=1, tiled=True),
        lax.all_to_all(d_qkv_all, "date", split_axis=0, concat_axis=1, tiled=True),
    )
    d_normed = back_normed(d_qkv, w_qkv)
    grad_in = norm_backward(grad_out, d_normed, normed, inv_std)
    token_rows = normed_b.shape[0] * normed_b.shape[1]
    left_inputs = normed_b.reshape(token_rows, width)
    right_inputs = d_qkv.reshape(token_rows, 3 * width)
    left_output = attn.reshape(token_rows, width)
    right_output = grad_out.reshape(token_rows, width)
    grad_qkv = lax.dot_general(
        left_inputs, right_inputs, (((0,), (0,)), ((), ())), preferred_element_type=jnp.float32
    )
    grad_proj = lax.dot_general(
        left_output, right_output, (((0,), (0,)), ((), ())), preferred_element_type=jnp.float32
    )
    weight_grad = lax.psum_scatter(
        jnp.concatenate([grad_qkv, grad_proj], axis=1),
        ("space", "date"),
        scatter_dimension=0,
        tiled=True,
    )
    return (grad_in, weight_grad)


def solution(mesh):
    return jax.shard_map(
        local,
        mesh=mesh,
        in_specs=(
            P("date", ("groups", "space"), None),
            P("date", ("groups", "space"), None),
            P(),
            P(),
            P(None, ("groups", "space", "date")),
        ),
        out_specs=(P("date", ("groups", "space"), None), P(("groups", "space", "date"), None)),
        check_vma=False,
    )
```

profile of v0, /device:TPU:0, one launch (start us, length us, event | category | flops | bytes accessed | tf_op | source)
XLA Modules:
  0.0 304.5 jit_solution(4945225939354096947)
XLA Ops:
  7.2 0.0 copy-start
  7.2 2.5 convolution_convert_fusion.3
  9.7 1.3 copy.58
  11.0 4.2 %all-to-all-start.1 = ((bf16[16,32,768]{2,0,1:T(8,128)(2,1)}), bf16[16,32,768]{2,0,1:T(8,128)(2,1)}, u32[]{:S(2)}, u32[]{:S(2)}) async-start(bf16[16,32,768]{2,0,1:T(8,128)(2,1)} %copy.58), calls=%async_computation.1 | async-start | bytes 1572864 | tf_op jit(solution)/shard_map/all_to_all | solution.py:104
  15.2 1.3 convert_reduce_fusion
  16.5 1.5 fusion.31
  18.0 1.4 fusion.19
  19.4 0.0 copy-start.5
  19.4 0.0 copy-done
  19.4 2.0 convolution_convert_fusion
  21.4 0.0 copy-done.5
  21.4 2.7 copy.53
  24.1 3.4 %all-to-all-done.1 = bf16[16,32,768]{2,0,1:T(8,128)(2,1)} async-done(((bf16[16,32,768]{2,0,1:T(8,128)(2,1)}), bf16[16,32,768]{2,0,1:T(8,128)(2,1)}, u32[]{:S(2)}, u32[]{:S(2)}) %all-to-all-start.1) | async-done | bytes 786464 | tf_op jit(solution)/shard_map/all_to_all | solution.py:104
  27.5 4.7 %all-to-all-start = ((bf16[16,32,2304]{2,0,1:T(8,128)(2,1)}), bf16[16,32,2304]{2,0,1:T(8,128)(2,1)}, u32[]{:S(2)}, u32[]{:S(2)}) async-start(bf16[16,32,2304]{2,0,1:T(8,128)(2,1)} %copy.53), calls=%async_computation | async-start | bytes 4718592 | tf_op jit(solution)/shard_map/all_to_all | solution.py:103
  32.2 0.7 compare_bitcast_fusion
  32.9 0.8 broadcast_or_fusion
  33.6 2.2 copy.60
  35.9 3.8 %reshape.92 = bf16[64,8,12,64]{3,2,1,0:T(8,128)(2,1)} reshape(bf16[4,16,8,768]{3,2,1,0:T(8,128)(2,1)} %copy.60) | data formatting | bytes 1572864 | tf_op jit(solution)/shard_map/reshape | solution.py:29
  39.7 4.1 %copy.67 = bf16[64,8,12,64]{0,3,2,1:T(8,128)(2,1)} copy(bf16[64,8,12,64]{3,2,1,0:T(8,128)(2,1)} %reshape.92) | data formatting | bytes 1572864 | tf_op jit(solution)/shard_map/reshape | solution.py:29
  43.8 16.8 %all-to-all-done = bf16[16,32,2304]{2,0,1:T(8,128)(2,1)} async-done(((bf16[16,32,2304]{2,0,1:T(8,128)(2,1)}), bf16[16,32,2304]{2,0,1:T(8,128)(2,1)}, u32[]{:S(2)}, u32[]{:S(2)}) %all-to-all-start) | async-done | bytes 2359328 | tf_op jit(solution)/shard_map/all_to_all | solution.py:103
  60.6 3.8 %copy.55 = bf16[4,16,8,2304]{3,2,1,0:T(8,128)(2,1)} copy(bf16[4,16,8,2304]{3,1,2,0:T(8,128)(2,1)} %bitcast.4) | data formatting | bytes 4718592 | tf_op jit(solution)/shard_map/all_to_all | solution.py:103
  64.3 8.2 %reshape.89 = bf16[64,8,3,12,64]{4,3,2,1,0:T(8,128)(2,1)} reshape(bf16[4,16,8,2304]{3,2,1,0:T(8,128)(2,1)} %copy.55) | data formatting | bytes 4718592 | tf_op jit(solution)/shard_map/reshape | solution.py:25
  72.5 0.0 copy-start.4
  72.5 5.7 %fusion.56 = (bf16[64,8,1,12,64]{4,3,2,1,0:T(8,128)(2,1)S(1)}, bf16[64,8,1,12,64]{4,3,2,1,0:T(8,128)(2,1)S(1)}, bf16[64,8,1,12,64]{4,3,2,1,0:T(8,128)(2,1)S(1)}) fusion(bf16[64,8,3,12,64]{4,3,2,1,0:T(8,128)(2,1)} %reshape.89), kind=kLoop, calls=%fused_computation.65 | loop fusion | bytes 4718592 | tf_op jit(solution)/shard_map/slice | solution.py:28
  78.2 0.0 copy-start.2
  78.2 0.0 copy-start.3
  78.2 0.0 copy-done.4
  78.2 3.0 fusion.45
  81.2 0.0 copy-done.2
  81.2 0.0 copy-done.3
  81.2 1.9 fusion.44
  83.2 0.0 copy-done.8
  83.2 1.3 fusion.57
  84.4 0.0 copy-start.9
  84.5 0.0 copy-start.10
  84.5 2.5 convolution_convert_fusion.1
  86.9 0.0 copy-done.9
  86.9 0.0 copy-done.10
  86.9 2.1 fusion.37
  89.0 2.6 copy.74
  91.6 4.4 %all-to-all-start.3 = ((bf16[64,8,768]{2,1,0:T(8,128)(2,1)}), bf16[64,8,768]{2,1,0:T(8,128)(2,1)}, u32[]{:S(2)}, u32[]{:S(2)}) async-start(bf16[64,8,768]{2,1,0:T(8,128)(2,1)} %copy.74), calls=%async_computation.3 | async-start | bytes 1572864 | tf_op jit(solution)/shard_map/all_to_all | solution.py:108
  96.0 8.7 %fusion.38 = bf16[64,8,1,12,64]{0,4,3,1,2:T(8,128)(2,1)} fusion(f32[8,12,64,64]{2,3,1,0:T(8,128)} %fusion.45, bf16[64,8,1,12,64]{4,3,2,1,0:T(8,128)(2,1)} %copy-done.3, f32[8,12,64,64]{2,3,1,0:T(8,128)} %copy-done.9, f32[8,12,64]{2,1,0:T(8,128)} %copy-done.10), kind=kOutput, calls=%fused_computation.43 | convolution fusion | flops 53483584 | bytes 4743168 | tf_op jit(solution)/shard_map/phtu,tphd->uphd/dot_general | solution.py:48
  104.8 8.2 %fusion.41 = bf16[64,8,1,12,64]{0,4,3,1,2:T(8,128)(2,1)} fusion(f32[8,12,64,64]{2,3,1,0:T(8,128)} %fusion.45, bf16[64,8,1,12,64]{4,3,2,1,0:T(8,128)(2,1)} %copy-done.2, f32[8,12,64,64]{2,3,1,0:T(8,128)} %copy-done.9, f32[8,12,64]{2,1,0:T(8,128)} %copy-done.10), kind=kOutput, calls=%fused_computation.44 | convolution fusion | flops 53483584 | bytes 4743168 | tf_op jit(solution)/shard_map/phtu,uphd->tphd/dot_general | solution.py:45
  113.0 5.7 %pad_maximum_fusion.1 = bf16[64,8,3,12,64]{0,4,3,1,2:T(8,128)(2,1)} fusion(bf16[64,8,1,12,64]{0,4,3,1,2:T(8,128)(2,1)} %fusion.37, bf16[64,8,1,12,64]{0,4,3,1,2:T(8,128)(2,1)} %fusion.38, bf16[64,8,1,12,64]{0,4,3,1,2:T(8,128)(2,1)} %fusion.41), kind=kLoop, calls=%fused_computation.3 | loop fusion | flops 2359296 | bytes 4718592 | tf_op jit(solution)/shard_map/stack | solution.py:54
  118.7 9.1 %copy.69 = bf16[64,8,3,12,64]{4,3,2,1,0:T(8,128)(2,1)} copy(bf16[64,8,3,12,64]{0,4,3,1,2:T(8,128)(2,1)} %pad_maximum_fusion.1) | data formatting | bytes 4718592 | tf_op jit(solution)/shard_map/stack | solution.py:54
  127.8 8.4 %reshape.93 = bf16[64,8,2304]{2,1,0:T(8,128)(2,1)} reshape(bf16[64,8,3,12,64]{4,3,2,1,0:T(8,128)(2,1)} %copy.69) | data formatting | bytes 4718592 | tf_op jit(solution)/shard_map/reshape | solution.py:54
  136.2 0.0 all-to-all-done.3
  136.2 4.5 %all-to-all-start.2 = ((bf16[64,8,2304]{2,1,0:T(8,128)(2,1)}), bf16[64,8,2304]{2,1,0:T(8,128)(2,1)}, u32[]{:S(2)}, u32[]{:S(2)}) async-start(bf16[64,8,2304]{2,1,0:T(8,128)(2,1)} %reshape.93), calls=%async_computation.2 | async-start | bytes 4718592 | tf_op jit(solution)/shard_map/all_to_all | solution.py:109
  140.7 0.3 reduce-scatter.2.cloned.1.call-start
  141.0 1.2 copy.75
  142.3 3.3 %fusion.59 = f32[768,768]{1,0:T(8,128)} fusion(bf16[512,768]{1,0:T(8,128)(2,1)S(1)} %bitcast.72, bf16[512,768]{1,0:T(8,128)(2,1)} %bitcast.76), kind=kOutput, calls=%fused_computation.68 | convolution fusion | flops 603979776 | bytes 3932160 | tf_op jit(solution)/shard_map/dot_general | solution.py:121
  145.6 23.7 %all-to-all-done.2 = bf16[64,8,2304]{2,1,0:T(8,128)(2,1)} async-done(((bf16[64,8,2304]{2,1,0:T(8,128)(2,1)}), bf16[64,8,2304]{2,1,0:T(8,128)(2,1)}, u32[]{:S(2)}, u32[]{:S(2)}) %all-to-all-start.2) | async-done | bytes 2359328 | tf_op jit(solution)/shard_map/all_to_all | solution.py:109
  169.3 2.0 copy.70
  171.3 0.0 copy-done.6
  171.3 4.9 %fusion.58 = f32[768,2304]{1,0:T(8,128)} fusion(bf16[512,768]{1,0:T(8,128)(2,1)S(1)} %bitcast.74, bf16[512,2304]{1,0:T(8,128)(2,1)S(1)} %bitcast.71), kind=kOutput, calls=%fused_computation.67 | convolution fusion | flops 1811939328 | bytes 10223616 | tf_op jit(solution)/shard_map/dot_general | solution.py:118
  176.2 8.7 %pad_maximum_fusion = f32[768,3072]{1,0:T(8,128)} fusion(f32[768,768]{1,0:T(8,128)} %fusion.59, f32[768,2304]{1,0:T(8,128)} %fusion.58), kind=kLoop, calls=%fused_computation.2 | loop fusion | flops 2359296 | bytes 18874368 | tf_op jit(solution)/shard_map/concatenate | solution.py:125
  184.9 0.0 reduce-scatter.2.cloned.1.call-update
  184.9 0.0 copy-start.1
  185.0 0.0 copy-start.7
  185.0 4.1 %fusion.55 = (f32[16,32]{1,0:T(8,128)S(1)}, f32[16,32]{1,0:T(8,128)S(1)}, f32[16,32,768]{2,1,0:T(8,128)S(1)}) fusion(f32[16,32]{1,0:T(8,128)S(1)} %add_rsqrt_fusion, f32[16,32]{1,0:T(8,128)S(1)} %broadcast_multiply_fusion.2, bf16[16,32,768]{2,1,0:T(8,128)(2,1)} %param.5, bf16[768,2304]{1,0:T(8,128)(2,1)S(1)} %copy-done, bf16[16,4,8,2304]{3,2,0,1:T(8,128)(2,1)} %bitcast.21), kind=kOutput, calls=%fused_computation.64 | convolution fusion | flops 1814297600 | bytes 8265728 | tf_op jit(solution)/shard_map/dot_general | solution.py:87
  189.1 0.0 copy-done.1
  189.1 0.0 copy-done.7
  189.1 1.5 fusion.30
  190.6 107.0 %reduce-scatter.2.cloned.1.call-done = f32[48,3072]{1,0:T(8,128)} async-done(((f32[768,3072]{1,0:T(8,128)}), f32[48,3072]{1,0:T(8,128)}) %reduce-scatter.2.cloned.1.call-update) | async-done | bytes 589840 | tf_op jit(solution)/shard_map/reduce_scatter | solution.py:124
  (6 shorter events, 0.0 us)
Async XLA Ops:
  7.2 12.2 %copy-start = (bf16[768,2304]{1,0:T(8,128)(2,1)S(1)}, bf16[768,2304]{1,0:T(8,128)(2,1)}, u32[]{:S(2)}) copy-start(bf16[768,2304]{1,0:T(8,128)(2,1)} %param.7) | copy-start | bytes 10616836
  11.0 16.5 %all-to-all-start.1 = ((bf16[16,32,768]{2,0,1:T(8,128)(2,1)}), bf16[16,32,768]{2,0,1:T(8,128)(2,1)}, u32[]{:S(2)}, u32[]{:S(2)}) async-start(bf16[16,32,768]{2,0,1:T(8,128)(2,1)} %copy.58), calls=%async_computation.1 | async-start | bytes 1572864 | tf_op jit(solution)/shard_map/all_to_all | solution.py:104
  19.4 2.0 copy-start.5
  27.5 33.1 %all-to-all-start = ((bf16[16,32,2304]{2,0,1:T(8,128)(2,1)}), bf16[16,32,2304]{2,0,1:T(8,128)(2,1)}, u32[]{:S(2)}, u32[]{:S(2)}) async-start(bf16[16,32,2304]{2,0,1:T(8,128)(2,1)} %copy.53), calls=%async_computation | async-start | bytes 4718592 | tf_op jit(solution)/shard_map/all_to_all | solution.py:103
  72.5 5.7 %copy-start.4 = (bf16[64,8,12,64]{0,3,2,1:T(8,128)(2,1)S(1)}, bf16[64,8,12,64]{0,3,2,1:T(8,128)(2,1)}, u32[]{:S(2)}) copy-start(bf16[64,8,12,64]{0,3,2,1:T(8,128)(2,1)} %copy.67) | copy-start | bytes 2359300
  78.2 3.0 copy-start.2
  78.2 3.0 copy-start.3
  81.2 1.9 copy-start.8
  84.4 2.5 copy-start.9
  84.5 2.5 copy-start.10
  91.6 44.6 %all-to-all-start.3 = ((bf16[64,8,768]{2,1,0:T(8,128)(2,1)}), bf16[64,8,768]{2,1,0:T(8,128)(2,1)}, u32[]{:S(2)}, u32[]{:S(2)}) async-start(bf16[64,8,768]{2,1,0:T(8,128)(2,1)} %copy.74), calls=%async_computation.3 | async-start | bytes 1572864 | tf_op jit(solution)/shard_map/all_to_all | solution.py:108
  136.2 33.1 %all-to-all-start.2 = ((bf16[64,8,2304]{2,1,0:T(8,128)(2,1)}), bf16[64,8,2304]{2,1,0:T(8,128)(2,1)}, u32[]{:S(2)}, u32[]{:S(2)}) async-start(bf16[64,8,2304]{2,1,0:T(8,128)(2,1)} %reshape.93), calls=%async_computation.2 | async-start | bytes 4718592 | tf_op jit(solution)/shard_map/all_to_all | solution.py:109
  140.7 156.9 %reduce-scatter.2.cloned.1.call-start = ((), (), s32[]{:S(2)}) async-start(), calls=%async_computation.5 | async-start | bytes 10027008 | tf_op jit(solution)/shard_map/reduce_scatter | solution.py:124
  169.3 2.0 copy-start.6
  184.9 4.1 %copy-start.1 = (bf16[16,32,768]{2,1,0:T(8,128)(2,1)S(1)}, bf16[16,32,768]{2,1,0:T(8,128)(2,1)}, u32[]{:S(2)}) copy-start(bf16[16,32,768]{2,1,0:T(8,128)(2,1)} %param.5) | copy-start | bytes 2359300
  185.0 4.1 %copy-start.7 = (bf16[16,32,768]{2,1,0:T(8,128)(2,1)S(1)}, bf16[16,32,768]{2,1,0:T(8,128)(2,1)}, u32[]{:S(2)}) copy-start(bf16[16,32,768]{2,1,0:T(8,128)(2,1)} %param.6) | copy-start | bytes 2359300
Sparse Core Ops, SparseCore 0:
  185.1 112.5 reduce-scatter.1
where the time goes:
time: 306 us; the launch traced here: 304 us
  waiting for transfers between devices  151 us (49%)
  local copies, waits for them, and re-layouts  55.1 us (18%)
  matrix products  43.2 us (14%)
  other arithmetic  22.9 us (7%)
  starting transfers between devices  18.1 us (6%)
  between operations  14.3 us (5%)
    reduce_scatter x1, waiting for transfers between devices, local(): lax.psum_scatter(jnp.concatenate([grad_qkv, grad_proj], axis=1), ('space'...  107 us
    all_to_all x1, waiting for transfers between devices, local(): lax.all_to_all(d_qkv_all, 'date', split_axis=0, concat_axis=1, tiled=True)  23.7 us
    all_to_all x1, waiting for transfers between devices, local(): lax.all_to_all(qkv_local, 'date', split_axis=1, concat_axis=0, tiled=True)  16.8 us
    another operation x1, local copies, waits for them, and re-layouts, attend(): jnp.stack([d_query, d_key, d_value], axis=2)  9.08 us
    concatenate x1, other arithmetic, local(): jnp.concatenate([grad_qkv, grad_proj], axis=1)  8.74 us
    dot_general x1, matrix products, attend(): jnp.einsum('phtu,tphd->uphd', d_score, query, preferred_element_type=jnp....  8.74 us
    reshape x1, local copies, waits for them, and re-layouts, attend(): jnp.stack([d_query, d_key, d_value], axis=2)  8.39 us
    dot_general x1, matrix products, attend(): jnp.einsum('phtu,uphd->tphd', d_score, keys, preferred_element_type=jnp.f...  8.25 us
  transfers between devices with their start and end apart: 5, of which 4 were waited for; matrix products, arithmetic and copies ran while one was open for 23% of the time, Pallas kernels for 0%

commit v1 on v0

v1 whole, which is shorter than its diff:
```python
import jax
import jax.numpy as jnp
from jax import lax
from jax.experimental import pallas as pl
from jax.experimental.pallas import tpu as pltpu
from jax.sharding import PartitionSpec as P

HD = 64
epsilon = 1e-05
F32 = jnp.float32
BF16 = jnp.bfloat16
NT = (((1,), (1,)), ((), ()))
TN = (((0,), (0,)), ((), ()))
ROWS = 128


def stats(rows):
    flat = rows.astype(F32)
    centred = flat - jnp.mean(flat, axis=-1, keepdims=True)
    variance = jnp.mean(centred * centred, axis=-1, keepdims=True)
    inv_std = lax.rsqrt(variance + epsilon)
    return centred * inv_std, inv_std


def group_rows(ref, i):
    dates, width = ref.shape[1:]
    n = ROWS // dates
    return ref[pl.ds(i * n, n)].reshape(ROWS, width)


def project(i, f_ref, g_ref, wq_ref, wo_ref, nbt, qkv, da):
    normed, _ = stats(group_rows(f_ref, i))
    nb = normed.astype(BF16)
    at = pl.ds(pl.multiple_of(i * ROWS, ROWS), ROWS)
    nbt[:, at] = nb.T
    qkv[at, :] = jnp.dot(nb, wq_ref[...], preferred_element_type=F32).astype(BF16)
    da[at, :] = lax.dot_general(
        group_rows(g_ref, i), wo_ref[...], NT, preferred_element_type=F32
    ).astype(BF16)


def attend(i, dates, vd_ref, qkv, da, att, dqkv):
    width = da.shape[1]
    scale = 1.0 / HD**0.5
    at = pl.ds(pl.multiple_of(i * ROWS, ROWS), ROWS)
    row = lax.broadcasted_iota(jnp.int32, (ROWS, ROWS), 0)
    col = lax.broadcasted_iota(jnp.int32, (ROWS, ROWS), 1)
    keep = ((row // dates) == (col // dates)) & ((vd_ref[i] == 1) | (row == col))
    bias = jnp.where(keep, 0.0, -1e30).astype(F32)
    bias = jnp.concatenate([bias, bias], axis=0)
    lane = lax.broadcasted_iota(jnp.int32, (1, 2 * HD), 1)
    first = jnp.where(lane < HD, 1.0, 0.0).astype(BF16)
    second = jnp.where(lane < HD, 0.0, 1.0).astype(BF16)

    def stack(a):
        return jnp.concatenate([a * first, a * second], axis=0)

    def side(a):
        return jnp.concatenate([a[:ROWS], a[ROWS:]], axis=1)

    for c in range(0, width, 2 * HD):
        q = stack(qkv[at, c : c + 2 * HD])
        k = qkv[at, width + c : width + c + 2 * HD]
        v = qkv[at, 2 * width + c : 2 * width + c + 2 * HD]
        d = stack(da[at, c : c + 2 * HD])
        s = lax.dot_general(q, k, NT, preferred_element_type=F32) * scale + bias
        e = jnp.exp(s - jnp.max(s, axis=-1, keepdims=True))
        prob = e / jnp.sum(e, axis=-1, keepdims=True)
        prob_b = prob.astype(BF16)
        o = jnp.dot(side(prob_b), stack(v), preferred_element_type=F32).astype(BF16)
        att[c : c + 2 * HD, at] = o.T
        dp = lax.dot_general(d, v, NT, preferred_element_type=F32)
        delta = jnp.sum(prob * dp, axis=-1, keepdims=True)
        ds = (prob * (dp - delta) * scale).astype(BF16)
        dqkv[at, c : c + 2 * HD] = jnp.dot(
            side(ds), stack(k), preferred_element_type=F32
        ).astype(BF16)
        dqkv[at, width + c : width + c + 2 * HD] = lax.dot_general(
            ds, q, TN, preferred_element_type=F32
        ).astype(BF16)
        dqkv[at, 2 * width + c : 2 * width + c + 2 * HD] = lax.dot_general(
            prob_b, d, TN, preferred_element_type=F32
        ).astype(BF16)


def norm_backward(i, f_ref, g_ref, wq_ref, dqkv):
    at = pl.ds(pl.multiple_of(i * ROWS, ROWS), ROWS)
    dn = lax.dot_general(dqkv[at, :], wq_ref[...], NT, preferred_element_type=F32)
    normed, inv_std = stats(group_rows(f_ref, i))
    first = jnp.mean(dn, axis=-1, keepdims=True)
    second = jnp.mean(dn * normed, axis=-1, keepdims=True)
    return (group_rows(g_ref, i).astype(F32) + inv_std * (dn - first - normed * second)).astype(
        BF16
    )


def compute_kernel(f_ref, g_ref, wq_ref, wo_ref, vd_ref, gi_ref, wg_ref, nbt, qkv, da, att, dqkv):
    patches, dates, width = f_ref.shape
    groups = patches * dates // ROWS
    n = ROWS // dates

    @pl.loop(0, groups)
    def _(i):
        project(i, f_ref, g_ref, wq_ref, wo_ref, nbt, qkv, da)
        attend(i, dates, vd_ref, qkv, da, att, dqkv)
        gi_ref[pl.ds(i * n, n)] = norm_backward(i, f_ref, g_ref, wq_ref, dqkv).reshape(
            n, dates, width
        )

    tile = 256

    @pl.loop(0, 3 * width // tile)
    def _(j):
        at = pl.ds(pl.multiple_of(j * tile, tile), tile)
        wg_ref[:, at] = jnp.dot(nbt[...], dqkv[:, at], preferred_element_type=F32).astype(BF16)

    for j in range(0, width, tile):
        g = g_ref[:, :, j : j + tile].reshape(patches * dates, tile)
        wg_ref[:, 3 * width + j : 3 * width + j + tile] = jnp.dot(
            att[...], g, preferred_element_type=F32
        ).astype(BF16)


def local(features, grad_out, w_qkv, w_out, valid_dates):
    width = features.shape[-1]
    dates, patches = valid_dates.shape
    tokens = dates * patches
    f = lax.all_to_all(features.transpose(1, 0, 2), "date", split_axis=0, concat_axis=1, tiled=True)
    g = lax.all_to_all(grad_out.transpose(1, 0, 2), "date", split_axis=0, concat_axis=1, tiled=True)
    vd = valid_dates.T.reshape(tokens // ROWS, 1, ROWS)
    vmem = pl.BlockSpec(memory_space=pltpu.VMEM)
    gi, wg = pl.pallas_call(
        compute_kernel,
        out_shape=(
            jax.ShapeDtypeStruct((patches, dates, width), BF16),
            jax.ShapeDtypeStruct((width, 4 * width), BF16),
        ),
        in_specs=[vmem] * 5,
        out_specs=(vmem, vmem),
        scratch_shapes=[
            pltpu.VMEM((width, tokens), BF16),
            pltpu.VMEM((tokens, 3 * width), BF16),
            pltpu.VMEM((tokens, width), BF16),
            pltpu.VMEM((width, tokens), BF16),
            pltpu.VMEM((tokens, 3 * width), BF16),
        ],
        compiler_params=pltpu.CompilerParams(vmem_limit_bytes=50 * 2**20),
    )(f, g, w_qkv, w_out, vd)
    weight_grad = lax.psum_scatter(wg, ("space", "date"), scatter_dimension=0, tiled=True)
    grad_in = lax.all_to_all(gi, "date", split_axis=1, concat_axis=0, tiled=True)
    return (grad_in.transpose(1, 0, 2), weight_grad.astype(F32))


def solution(mesh):
    return jax.shard_map(
        local,
        mesh=mesh,
        in_specs=(
            P("date", ("groups", "space"), None),
            P("date", ("groups", "space"), None),
            P(),
            P(),
            P(None, ("groups", "space", "date")),
        ),
        out_specs=(P("date", ("groups", "space"), None), P(("groups", "space", "date"), None)),
        check_vma=False,
    )
```

time: 306 us -> 159 us (0.52)
  waiting for transfers between devices: 151 us -> 83 us
  local copies, waits for them, and re-layouts: 55.1 us -> 5.46 us
  matrix products: 43.2 us -> 0 us
  Pallas kernels: 0 us -> 32.3 us
  other arithmetic: 22.9 us -> 1.81 us
  blocking collectives: 0 us -> 14.1 us
  starting transfers between devices: 18.1 us -> 7.74 us
    reduce_scatter x1, waiting for transfers between devices: 107 us -> 61.3 us  [local(): lax.psum_scatter(wg, ('space', 'date'), scatter_dimension=0, tiled=True)]
    dot_general x11 -> x0, matrix products: 43.2 us -> none  [the longest x1 8.74 us: attend(): jnp.einsum('phtu,tphd->uphd', d_score, query, preferred_element_type=jnp....]
    pallas_call x0 -> x1, Pallas kernels: none -> 32.3 us  [local(): pl.pallas_call(compute_kernel, out_shape=(jax.ShapeDtypeStruct((patches,...]
    reshape x7 -> x1, local copies, waits for them, and re-layouts: 31.1 us -> 0.08 us  [local(): vd = valid_dates.T.reshape(tokens // ROWS, 1, ROWS)]
    all_to_all x4 -> x2, waiting for transfers between devices: 43.8 us -> 21.7 us  [the longest x1 11.4 us: local(): lax.all_to_all(grad_out.transpose(1, 0, 2), 'date', split_axis=0, concat_...]
    all_to_all x0 -> x1, blocking collectives: none -> 14.1 us  [local(): lax.all_to_all(gi, 'date', split_axis=1, concat_axis=0, tiled=True)]
    all_to_all x4 -> x2, starting transfers between devices: 17.8 us -> 7.7 us  [the longest x1 4.21 us: local(): lax.all_to_all(features.transpose(1, 0, 2), 'date', split_axis=0, concat_...]
    another operation x1 -> x0, local copies, waits for them, and re-layouts: 9.08 us -> none  [attend(): jnp.stack([d_query, d_key, d_value], axis=2)]
  transfers between devices with their start and end apart: 5 -> 3, of which waited for: 4 -> 3; matrix products, arithmetic and copies ran while one was open for 23% -> 2% of each run, Pallas kernels for 0% -> 0%
where the time goes in v1:
time: 159 us
  waiting for transfers between devices  83 us (52%)
  Pallas kernels  32.3 us (20%)
  blocking collectives  14.1 us (9%)
  between operations  14.1 us (9%)
  starting transfers between devices  7.74 us (5%)
  local copies, waits for them, and re-layouts  5.46 us (3%)
  other arithmetic  1.81 us (1%)
    reduce_scatter x1, waiting for transfers between devices, local(): lax.psum_scatter(wg, ('space', 'date'), scatter_dimension=0, tiled=True)  61.3 us
    pallas_call x1, Pallas kernels, local(): pl.pallas_call(compute_kernel, out_shape=(jax.ShapeDtypeStruct((patches,...  32.3 us
    all_to_all x1, blocking collectives, local(): lax.all_to_all(gi, 'date', split_axis=1, concat_axis=0, tiled=True)  14.1 us
    all_to_all x1, waiting for transfers between devices, local(): lax.all_to_all(grad_out.transpose(1, 0, 2), 'date', split_axis=0, concat_...  11.4 us
    all_to_all x1, waiting for transfers between devices, local(): lax.all_to_all(features.transpose(1, 0, 2), 'date', split_axis=0, concat_...  10.3 us
    all_to_all x1, starting transfers between devices, local(): lax.all_to_all(features.transpose(1, 0, 2), 'date', split_axis=0, concat_...  4.21 us
    unnamed x8, local copies, waits for them, and re-layouts  3.85 us
    all_to_all x1, starting transfers between devices, local(): lax.all_to_all(grad_out.transpose(1, 0, 2), 'date', split_axis=0, concat_...  3.49 us
  transfers between devices with their start and end apart: 3, of which 3 were waited for; matrix products, arithmetic and copies ran while one was open for 2% of the time, Pallas kernels for 0%

profile of v1, /device:TPU:0, one launch (start us, length us, event | category | flops | bytes accessed | tf_op | source)
XLA Modules:
  0.0 158.5 jit_solution(14090484061060645048)
XLA Ops:
  7.2 0.0 copy-start.1
  7.2 0.0 copy-start.2
  7.2 2.5 %copy.21 = bf16[16,32,768]{2,0,1:T(8,128)(2,1)} copy(bf16[16,32,768]{2,1,0:T(8,128)(2,1)} %param.5) | data formatting | bytes 1572864 | tf_op args[0]
  9.7 4.2 %all-to-all-start = ((bf16[32,16,768]{2,1,0:T(8,128)(2,1)}), bf16[32,16,768]{2,1,0:T(8,128)(2,1)S(1)}, u32[]{:S(2)}, u32[]{:S(2)}) async-start(bf16[32,16,768]{2,1,0:T(8,128)(2,1)} %bitcast.22), calls=%async_computation | async-start | bytes 1572864 | tf_op jit(solution)/shard_map/all_to_all | solution.py:128
  13.9 0.0 copy-done.1
  13.9 0.0 copy-start
  13.9 1.3 copy.20
  15.2 10.3 %all-to-all-done = bf16[32,16,768]{2,1,0:T(8,128)(2,1)S(1)} async-done(((bf16[32,16,768]{2,1,0:T(8,128)(2,1)}), bf16[32,16,768]{2,1,0:T(8,128)(2,1)S(1)}, u32[]{:S(2)}, u32[]{:S(2)}) %all-to-all-start) | async-done | bytes 786464 | tf_op jit(solution)/shard_map/all_to_all | solution.py:128
  25.6 3.5 %all-to-all-start.1 = ((bf16[32,16,768]{2,1,0:T(8,128)(2,1)}), bf16[32,16,768]{2,1,0:T(8,128)(2,1)S(1)}, u32[]{:S(2)}, u32[]{:S(2)}) async-start(bf16[32,16,768]{2,1,0:T(8,128)(2,1)} %bitcast.21), calls=%async_computation.1 | async-start | bytes 1572864 | tf_op jit(solution)/shard_map/all_to_all | solution.py:129
  29.1 0.0 reduce-scatter.2.cloned.1.call-start
  29.1 0.0 copy-done.2
  29.1 0.1 reshape.7.vd_ref
  29.2 0.1 copy.11
  29.3 11.4 %all-to-all-done.1 = bf16[32,16,768]{2,1,0:T(8,128)(2,1)S(1)} async-done(((bf16[32,16,768]{2,1,0:T(8,128)(2,1)}), bf16[32,16,768]{2,1,0:T(8,128)(2,1)S(1)}, u32[]{:S(2)}, u32[]{:S(2)}) %all-to-all-start.1) | async-done | bytes 786464 | tf_op jit(solution)/shard_map/all_to_all | solution.py:129
  40.7 0.1 copy.13
  40.8 0.0 copy-done
  40.8 32.3 %shard_map.68 = (bf16[8,64,768]{2,1,0:T(8,128)(2,1)S(1)}, bf16[768,3072]{1,0:T(8,128)(2,1)}) custom-call(bf16[8,64,768]{2,1,0:T(8,128)(2,1)S(1)} %bitcast.23, bf16[8,64,768]{2,1,0:T(8,128)(2,1)S(1)} %bitcast.24, bf16[768,2304]{1,0:T(8,128)(2,1)} %wq_ref.1, bf16[768,768]{1,0:T(8,128)(2,1)S(1)} %copy-done, s32[4,1,128]{2,1,0:T(1,128)S(1)} %reshape.7.vd_ref), custom_call_target="tpu_custom_call" | custom-call | tf_op jit(solution)/shard_map/pallas_call | solution.py:132
  73.1 0.0 reduce-scatter.2.cloned.1.call-update
  73.1 0.4 copy.14
  73.6 14.1 %all_to_all.54 = bf16[8,64,768]{2,0,1:T(8,128)(2,1)S(1)} all-to-all(bf16[8,64,768]{2,0,1:T(8,128)(2,1)S(1)} %copy.14), channel_id=1, replica_groups=mesh['groups'=2,'space'=4,'date'=4] {'date'}, dimensions={1} | all-to-all | bytes 1572864 | tf_op jit(solution)/shard_map/all_to_all | solution.py:150
  87.6 1.0 copy.19
  88.6 61.3 %reduce-scatter.2.cloned.1.call-done = bf16[48,3072]{1,0:T(8,128)(2,1)} async-done(((bf16[768,3072]{1,0:T(8,128)(2,1)}), bf16[48,3072]{1,0:T(8,128)(2,1)}) %reduce-scatter.2.cloned.1.call-update) | async-done | bytes 294928 | tf_op jit(solution)/shard_map/reduce_scatter | solution.py:149
  149.9 1.8 %convert_element_type.3 = f32[48,3072]{1,0:T(8,128)} convert(bf16[48,3072]{1,0:T(8,128)(2,1)} %reduce-scatter.2.cloned.1.call-done) | non-fusion elementwise | flops 147456 | bytes 884736 | tf_op jit(solution)/shard_map/convert_element_type | solution.py:151
Async XLA Ops:
  7.2 6.7 %copy-start.1 = (bf16[16,32,768]{2,1,0:T(8,128)(2,1)S(1)}, bf16[16,32,768]{2,1,0:T(8,128)(2,1)}, u32[]{:S(2)}) copy-start(bf16[16,32,768]{2,1,0:T(8,128)(2,1)} %param.6) | copy-start | bytes 2359300
  7.2 21.9 %copy-start.2 = (s32[64,8]{0,1:T(8,128)S(1)}, s32[64,8]{0,1:T(8,128)}, u32[]{:S(2)}) copy-start(s32[64,8]{0,1:T(8,128)} %param.9) | copy-start | bytes 6148
  9.7 15.9 %all-to-all-start = ((bf16[32,16,768]{2,1,0:T(8,128)(2,1)}), bf16[32,16,768]{2,1,0:T(8,128)(2,1)S(1)}, u32[]{:S(2)}, u32[]{:S(2)}) async-start(bf16[32,16,768]{2,1,0:T(8,128)(2,1)} %bitcast.22), calls=%async_computation | async-start | bytes 1572864 | tf_op jit(solution)/shard_map/all_to_all | solution.py:128
  13.9 26.9 %copy-start = (bf16[768,768]{1,0:T(8,128)(2,1)S(1)}, bf16[768,768]{1,0:T(8,128)(2,1)}, u32[]{:S(2)}) copy-start(bf16[768,768]{1,0:T(8,128)(2,1)} %wo_ref.1) | copy-start | bytes 3538948
  25.6 15.1 %all-to-all-start.1 = ((bf16[32,16,768]{2,1,0:T(8,128)(2,1)}), bf16[32,16,768]{2,1,0:T(8,128)(2,1)S(1)}, u32[]{:S(2)}, u32[]{:S(2)}) async-start(bf16[32,16,768]{2,1,0:T(8,128)(2,1)} %bitcast.21), calls=%async_computation.1 | async-start | bytes 1572864 | tf_op jit(solution)/shard_map/all_to_all | solution.py:129
  29.1 120.8 %reduce-scatter.2.cloned.1.call-start = ((), (), s32[]{:S(2)}) async-start(), calls=%async_computation.4 | async-start | bytes 5013504 | tf_op jit(solution)/shard_map/reduce_scatter | solution.py:149
Sparse Core Ops, SparseCore 0:
  73.2 76.5 reduce-scatter.1

commit v2 on v1

--- a/solution.py
+++ b/solution.py
@@ -121,7 +121,7 @@
         ).astype(BF16)
 
 
-def local(features, grad_out, w_qkv, w_out, valid_dates):
+def local_plain(features, grad_out, w_qkv, w_out, valid_dates):
     width = features.shape[-1]
     dates, patches = valid_dates.shape
     tokens = dates * patches
@@ -151,6 +151,258 @@
     return (grad_in.transpose(1, 0, 2), weight_grad.astype(F32))
 
 
+TILE = 256
+LAG = 2
+MESH = pl.DeviceIdType.MESH
+
+
+def full_kernel(
+    f_in, g_in, wq_in, wo_in, vd_ref, gi_out, wg_out,
+    f_ref, g_ref, wq_ref, wo_ref, nbt, qkv, da, att, dqkv, gi, part, core_in, core_sum, x_in, x_sum, z_in,
+    load_sem, fs, fr, gs, gr, cs, cr, xs, xr, zs, zr,
+):
+    patches, dates, width = f_ref.shape
+    near = f_in.shape[1]
+    groups = patches * dates // ROWS
+    n = ROWS // dates
+    chunks = part.shape[0]
+    spaces = x_sum.shape[1]
+    inner = 3 * width // TILE
+    date = lax.axis_index("date")
+    space = lax.axis_index("space")
+    core = lax.rem(date, 2)
+    chip = date // 2
+    peers = (date + 1 - 2 * core, lax.rem(date + 2, 4), 3 - date)
+
+    def spaced(k):
+        return lax.rem(space + k, spaces)
+
+    barrier = pltpu.get_barrier_semaphore()
+    for peer in peers:
+        pl.semaphore_signal(barrier, inc=1, device_id={"date": peer}, device_id_type=MESH)
+    for k in range(1, spaces):
+        pl.semaphore_signal(barrier, inc=1, device_id={"space": spaced(k)}, device_id_type=MESH)
+
+    here = pl.ds(pl.multiple_of(date * near, near), near)
+    mine = pl.ds(date * patches, patches)
+    loads = [
+        pltpu.make_async_copy(f_in.at[mine], f_ref.at[:, here], load_sem.at[0]),
+        pltpu.make_async_copy(g_in.at[mine], g_ref.at[:, here], load_sem.at[1]),
+        pltpu.make_async_copy(wq_in, wq_ref, load_sem.at[2]),
+        pltpu.make_async_copy(wo_in, wo_ref, load_sem.at[3]),
+    ]
+    for copy in loads:
+        copy.start()
+    pl.semaphore_wait(barrier, 2 + spaces)
+
+    def forward(i, r, a):
+        src, dst = ((f_in, f_ref), (g_in, g_ref))[a]
+        return pltpu.make_async_remote_copy(
+            src_ref=src.at[pl.ds(peers[r] * patches + i * n, n)],
+            dst_ref=dst.at[pl.ds(i * n, n), here],
+            send_sem=fs.at[i, r, a],
+            recv_sem=fr.at[i, r, a],
+            device_id={"date": peers[r]},
+            device_id_type=MESH,
+        )
+
+    def backward(i, r):
+        there = pl.ds(pl.multiple_of(peers[r] * near, near), near)
+        return pltpu.make_async_remote_copy(
+            src_ref=gi.at[pl.ds(i * n, n), there],
+            dst_ref=gi_out.at[pl.ds(date * patches + i * n, n)],
+            send_sem=gs.at[i, r],
+            recv_sem=gr.at[i, r],
+            device_id={"date": peers[r]},
+            device_id_type=MESH,
+        )
+
+    def over_core(j):
+        return pltpu.make_async_remote_copy(
+            src_ref=part.at[j, :, :, 1 - core],
+            dst_ref=core_in.at[j],
+            send_sem=cs.at[j],
+            recv_sem=cr.at[j],
+            device_id={"date": peers[0]},
+            device_id_type=MESH,
+        )
+
+    def over_chip(j):
+        return pltpu.make_async_remote_copy(
+            src_ref=core_sum.at[j, :, 1 - chip],
+            dst_ref=x_in.at[j],
+            send_sem=xs.at[j],
+            recv_sem=xr.at[j],
+            device_id={"date": peers[1]},
+            device_id_type=MESH,
+        )
+
+    def over_space(j, k):
+        return pltpu.make_async_remote_copy(
+            src_ref=x_sum.at[j, spaced(k)],
+            dst_ref=z_in.at[j, k - 1],
+            send_sem=zs.at[j, k - 1],
+            recv_sem=zr.at[j, k - 1],
+            device_id={"space": spaced(k)},
+            device_id_type=MESH,
+        )
+
+    @pl.loop(0, groups)
+    def _(i):
+        for r in (1, 2, 0):
+            for a in range(2):
+                forward(i, r, a).start()
+
+    for copy in loads:
+        copy.wait()
+
+    @pl.loop(0, groups)
+    def _(i):
+        for r in range(3):
+            for a in range(2):
+                forward(i, r, a).wait_recv()
+        project(i, f_ref, g_ref, wq_ref, wo_ref, nbt, qkv, da)
+        attend(i, dates, vd_ref, qkv, da, att, dqkv)
+
+    @pl.loop(0, chunks + LAG)
+    def _(j):
+        @pl.when(j < inner)
+        def _():
+            at = pl.ds(pl.multiple_of(j * TILE, TILE), TILE)
+            w = jnp.dot(nbt[...], dqkv[:, at], preferred_element_type=F32).astype(BF16)
+            part[j] = w.reshape(part.shape[1:])
+
+        @pl.when((j >= inner) & (j < chunks))
+        def _():
+            at = pl.ds(pl.multiple_of((j - inner) * TILE, TILE), TILE)
+            g = g_ref[:, :, at].reshape(patches * dates, TILE)
+            w = jnp.dot(att[...], g, preferred_element_type=F32).astype(BF16)
+            part[j] = w.reshape(part.shape[1:])
+
+        @pl.when(j < chunks)
+        def _():
+            over_core(j).start()
+
+        @pl.when(j >= LAG)
+        def _():
+            b = j - LAG
+            over_core(b).wait_recv()
+            total = part[b, :, :, core].astype(F32) + core_in[b].astype(F32)
+            core_sum[b] = total.astype(BF16)
+            over_chip(b).start()
+
+    share = chunks // groups
+
+    @pl.loop(0, groups)
+    def _(i):
+        gi[pl.ds(i * n, n)] = norm_backward(i, f_ref, g_ref, wq_ref, dqkv).reshape(n, dates, width)
+        for r in (1, 2, 0):
+            backward(i, r).start()
+
+        @pl.loop(i * share, (i + 1) * share)
+        def _(j):
+            over_chip(j).wait_recv()
+            total = core_sum[j, :, chip].astype(F32) + x_in[j].astype(F32)
+            x_sum[j] = total.astype(BF16)
+            for k in range(1, spaces):
+                over_space(j, k).start()
+
+    own = pltpu.make_async_copy(gi.at[:, here], gi_out.at[mine], load_sem.at[0])
+    own.start()
+
+    @pl.loop(0, chunks)
+    def _(j):
+        total = x_sum[j, space].astype(F32)
+        for k in range(1, spaces):
+            over_space(j, k).wait_recv()
+            total += z_in[j, k - 1].astype(F32)
+        wg_out[:, pl.ds(pl.multiple_of(j * TILE, TILE), TILE)] = total
+        over_core(j).wait_send()
+        over_chip(j).wait_send()
+        for k in range(1, spaces):
+            over_space(j, k).wait_send()
+
+    own.wait()
+
+    @pl.loop(0, groups)
+    def _(i):
+        for r in range(3):
+            backward(i, r).wait()
+            for a in range(2):
+                forward(i, r, a).wait_send()
+
+
+def local_full(features, grad_out, w_qkv, w_out, valid_dates):
+    width = features.shape[-1]
+    dates, patches = valid_dates.shape
+    near, wide = features.shape[:2]
+    tokens = dates * patches
+    groups = tokens // ROWS
+    spaces = lax.axis_size("space")
+    chunks = 4 * width // TILE
+    rows = width // (4 * spaces)
+    vd = valid_dates.T.reshape(groups, 1, ROWS)
+    vmem = pl.BlockSpec(memory_space=pltpu.VMEM)
+    anywhere = pl.BlockSpec(memory_space=pl.ANY)
+    dma = pltpu.SemaphoreType.DMA
+    gi, wg = pl.pallas_call(
+        full_kernel,
+        out_shape=(
+            jax.ShapeDtypeStruct((wide, near, width), BF16),
+            jax.ShapeDtypeStruct((rows, 4 * width), F32),
+        ),
+        in_specs=[anywhere] * 4 + [vmem],
+        out_specs=(anywhere, vmem),
+        scratch_shapes=[
+            pltpu.VMEM((patches, dates, width), BF16),
+            pltpu.VMEM((patches, dates, width), BF16),
+            pltpu.VMEM((width, 3 * width), BF16),
+            pltpu.VMEM((width, width), BF16),
+            pltpu.VMEM((width, tokens), BF16),
+            pltpu.VMEM((tokens, 3 * width), BF16),
+            pltpu.VMEM((tokens, width), BF16),
+            pltpu.VMEM((width, tokens), BF16),
+            pltpu.VMEM((tokens, 3 * width), BF16),
+            pltpu.VMEM((patches, dates, width), BF16),
+            pltpu.VMEM((chunks, spaces, 2, 2, rows, TILE), BF16),
+            pltpu.VMEM((chunks, spaces, 2, rows, TILE), BF16),
+            pltpu.VMEM((chunks, spaces, 2, rows, TILE), BF16),
+            pltpu.VMEM((chunks, spaces, rows, TILE), BF16),
+            pltpu.VMEM((chunks, spaces, rows, TILE), BF16),
+            pltpu.VMEM((chunks, spaces - 1, rows, TILE), BF16),
+            dma((4,)),
+            dma((groups, 3, 2)),
+            dma((groups, 3, 2)),
+            dma((groups, 3)),
+            dma((groups, 3)),
+            dma((chunks,)),
+            dma((chunks,)),
+            dma((chunks,)),
+            dma((chunks,)),
+            dma((chunks, spaces - 1)),
+            dma((chunks, spaces - 1)),
+        ],
+        compiler_params=pltpu.CompilerParams(
+            collective_id=0, has_side_effects=True, vmem_limit_bytes=56 * 2**20
+        ),
+    )(features.transpose(1, 0, 2), grad_out.transpose(1, 0, 2), w_qkv, w_out, vd)
+    return (gi.transpose(1, 0, 2), wg)
+
+
+def local(features, grad_out, w_qkv, w_out, valid_dates):
+    width = features.shape[-1]
+    parts = 4 * lax.axis_size("space")
+    tokens = valid_dates.size
+    fits = (
+        lax.axis_size("date") == 4
+        and width % (16 * parts) == 0
+        and features.shape[0] % 16 == 0
+        and (4 * width // TILE) % (tokens // ROWS) == 0
+    )
+    way = local_full if fits else local_plain
+    return way(features, grad_out, w_qkv, w_out, valid_dates)
+
+
 def solution(mesh):
     return jax.shard_map(
         local,

time: 159 us -> 78.9 us (0.50)
  waiting for transfers between devices: 83 us -> 0 us
  Pallas kernels: 32.3 us -> 69.1 us
  blocking collectives: 14.1 us -> 0 us
  between operations: 14.1 us -> 0.64 us
  starting transfers between devices: 7.74 us -> 0 us
  local copies, waits for them, and re-layouts: 5.46 us -> 8.87 us
  other arithmetic: 1.81 us -> 0 us
    reduce_scatter x1 -> x0, waiting for transfers between devices: 61.3 us -> none  [local(): lax.psum_scatter(wg, ('space', 'date'), scatter_dimension=0, tiled=True)]
    pallas_call x1, Pallas kernels: 32.3 us -> 69.1 us  [local_full(): pl.pallas_call(full_kernel, out_shape=(jax.ShapeDtypeStruct((wide, near,...]
    all_to_all x2 -> x0, waiting for transfers between devices: 21.7 us -> none  [the longest x1 11.4 us: local(): lax.all_to_all(grad_out.transpose(1, 0, 2), 'date', split_axis=0, concat_...]
    all_to_all x1 -> x0, blocking collectives: 14.1 us -> none  [local(): lax.all_to_all(gi, 'date', split_axis=1, concat_axis=0, tiled=True)]
    all_to_all x2 -> x0, starting transfers between devices: 7.7 us -> none  [the longest x1 4.21 us: local(): lax.all_to_all(features.transpose(1, 0, 2), 'date', split_axis=0, concat_...]
    transpose x0 -> x1, local copies, waits for them, and re-layouts: none -> 3.37 us  [local_full(): grad_out.transpose(1, 0, 2)]
    convert_element_type x1 -> x0, other arithmetic: 1.81 us -> none  [local(): return (grad_in.transpose(1, 0, 2), weight_grad.astype(F32))]
    unnamed x8 -> x2, local copies, waits for them, and re-layouts: 3.85 us -> 4.16 us
  transfers between devices with their start and end apart: 3 -> 0, of which waited for: 3 -> 0; matrix products, arithmetic and copies ran while one was open for 2% -> 0% of each run, Pallas kernels for 0% -> 0%
where the time goes in v2:
time: 78.9 us; the launch traced here: 78.6 us
  Pallas kernels  69.1 us (88%)
  local copies, waits for them, and re-layouts  8.87 us (11%)
    pallas_call x1, Pallas kernels, local_full(): pl.pallas_call(full_kernel, out_shape=(jax.ShapeDtypeStruct((wide, near,...  69.1 us
    unnamed x2, local copies, waits for them, and re-layouts  4.16 us
    transpose x1, local copies, waits for them, and re-layouts, local_full(): grad_out.transpose(1, 0, 2)  3.37 us

profile of v2, /device:TPU:0, one launch (start us, length us, event | category | flops | bytes accessed | tf_op | source)
XLA Modules:
  0.0 78.6 jit_solution(13124580885606053077)
XLA Ops:
  0.6 1.3 %reshape.7.vd_ref = s32[4,1,128]{2,1,0:T(1,128)} reshape(s32[8,64]{1,0:T(8,128)} %bitcast.7) | data formatting | bytes 4096 | tf_op jit(solution)/shard_map/reshape | solution.py:344
  2.0 3.4 %copy_bitcast_fusion = (bf16[32,16,768]{2,1,0:T(8,128)(2,1)}, bf16[32,16,768]{2,1,0:T(8,128)(2,1)}) fusion(bf16[16,32,768]{2,1,0:T(8,128)(2,1)} %param.6, bf16[16,32,768]{2,1,0:T(8,128)(2,1)} %param.5), kind=kLoop, calls=%fused_computation | loop fusion | bytes 3145728 | tf_op jit(solution)/shard_map/transpose | solution.py:388
  5.3 69.1 %shard_map.68 = (bf16[32,16,768]{2,1,0:T(8,128)(2,1)}, f32[48,3072]{1,0:T(8,128)}) custom-call(bf16[32,16,768]{2,1,0:T(8,128)(2,1)} %get-tuple-element.9.f_in, bf16[32,16,768]{2,1,0:T(8,128)(2,1)} %get-tuple-element.8.g_in, bf16[768,2304]{1,0:T(8,128)(2,1)} %wq_in.1, bf16[768,768]{1,0:T(8,128)(2,1)} %wo_in.1, s32[4,1,128]{2,1,0:T(1,128)} %reshape.7.vd_ref), custom_call_target="tpu_custom_call" | custom-call | tf_op jit(solution)/shard_map/pallas_call | solution.py:348
  74.4 2.2 %copy.9 = bf16[16,32,768]{2,1,0:T(8,128)(2,1)} copy(bf16[16,32,768]{2,0,1:T(8,128)(2,1)} %bitcast.6) | data formatting | bytes 1572864
  76.6 1.9 %copy.13 = f32[48,3072]{1,0:T(8,128)} copy(f32[48,3072]{1,0:T(8,128)} %get-tuple-element.13) | data formatting | bytes 1179648

commit v3 on v2

--- a/solution.py
+++ b/solution.py
@@ -10,7 +10,6 @@
 F32 = jnp.float32
 BF16 = jnp.bfloat16
 NT = (((1,), (1,)), ((), ()))
-TN = (((0,), (0,)), ((), ()))
 ROWS = 128
 
 
@@ -43,43 +42,55 @@
     width = da.shape[1]
     scale = 1.0 / HD**0.5
     at = pl.ds(pl.multiple_of(i * ROWS, ROWS), ROWS)
+    n = ROWS // dates
+    patch = lax.broadcasted_iota(jnp.int32, vd_ref.shape, 1)
+    valid = vd_ref[...]
+    valid = jnp.concatenate(
+        [
+            jnp.sum(jnp.where(patch == i * n + p, valid, 0), axis=1, keepdims=True)
+            for p in range(n)
+        ],
+        axis=0,
+    )
     row = lax.broadcasted_iota(jnp.int32, (ROWS, ROWS), 0)
     col = lax.broadcasted_iota(jnp.int32, (ROWS, ROWS), 1)
-    keep = ((row // dates) == (col // dates)) & ((vd_ref[i] == 1) | (row == col))
+    keep = ((row // dates) == (col // dates)) & ((valid == 1) | (row == col))
     bias = jnp.where(keep, 0.0, -1e30).astype(F32)
-    bias = jnp.concatenate([bias, bias], axis=0)
+    bias = jnp.concatenate([bias, bias], axis=1)
     lane = lax.broadcasted_iota(jnp.int32, (1, 2 * HD), 1)
-    first = jnp.where(lane < HD, 1.0, 0.0).astype(BF16)
-    second = jnp.where(lane < HD, 0.0, 1.0).astype(BF16)
-
-    def stack(a):
-        return jnp.concatenate([a * first, a * second], axis=0)
-
-    def side(a):
-        return jnp.concatenate([a[:ROWS], a[ROWS:]], axis=1)
+    first = jnp.where(lane < HD, 1.0, 0.0)
+    second = jnp.where(lane < HD, 0.0, 1.0)
+    ones = (first.astype(BF16), second.astype(BF16))
+    scales = ((first * scale).astype(BF16), (second * scale).astype(BF16))
+
+    def stack(a, by):
+        return jnp.concatenate([a * by[0], a * by[1]], axis=0)
+
+    def halves(a):
+        return jnp.concatenate([a[:HD, :ROWS], a[HD:, ROWS:]], axis=0).astype(BF16)
 
     for c in range(0, width, 2 * HD):
-        q = stack(qkv[at, c : c + 2 * HD])
+        q = stack(qkv[at, c : c + 2 * HD], scales)
         k = qkv[at, width + c : width + c + 2 * HD]
         v = qkv[at, 2 * width + c : 2 * width + c + 2 * HD]
-        d = stack(da[at, c : c + 2 * HD])
-        s = lax.dot_general(q, k, NT, preferred_element_type=F32) * scale + bias
-        e = jnp.exp(s - jnp.max(s, axis=-1, keepdims=True))
-        prob = e / jnp.sum(e, axis=-1, keepdims=True)
+        d = stack(da[at, c : c + 2 * HD], ones)
+        s = lax.dot_general(k, q, NT, preferred_element_type=F32) + bias
+        e = jnp.exp(s - jnp.max(s, axis=0, keepdims=True))
+        prob = e * (1.0 / jnp.sum(e, axis=0, keepdims=True))
         prob_b = prob.astype(BF16)
-        o = jnp.dot(side(prob_b), stack(v), preferred_element_type=F32).astype(BF16)
-        att[c : c + 2 * HD, at] = o.T
-        dp = lax.dot_general(d, v, NT, preferred_element_type=F32)
-        delta = jnp.sum(prob * dp, axis=-1, keepdims=True)
-        ds = (prob * (dp - delta) * scale).astype(BF16)
-        dqkv[at, c : c + 2 * HD] = jnp.dot(
-            side(ds), stack(k), preferred_element_type=F32
+        att[c : c + 2 * HD, at] = halves(jnp.dot(v.T, prob_b, preferred_element_type=F32))
+        dp = lax.dot_general(v, d, NT, preferred_element_type=F32)
+        delta = jnp.sum(prob * dp, axis=0, keepdims=True)
+        ds = (prob * (dp - delta)).astype(BF16)
+        k_scaled = k * jnp.asarray(scale, BF16)
+        dqkv[at, c : c + 2 * HD] = halves(
+            jnp.dot(k_scaled.T, ds, preferred_element_type=F32)
+        ).T
+        dqkv[at, width + c : width + c + 2 * HD] = jnp.dot(
+            ds, q, preferred_element_type=F32
         ).astype(BF16)
-        dqkv[at, width + c : width + c + 2 * HD] = lax.dot_general(
-            ds, q, TN, preferred_element_type=F32
-        ).astype(BF16)
-        dqkv[at, 2 * width + c : 2 * width + c + 2 * HD] = lax.dot_general(
-            prob_b, d, TN, preferred_element_type=F32
+        dqkv[at, 2 * width + c : 2 * width + c + 2 * HD] = jnp.dot(
+            prob_b, d, preferred_element_type=F32
         ).astype(BF16)
 
 
@@ -127,7 +138,6 @@
     tokens = dates * patches
     f = lax.all_to_all(features.transpose(1, 0, 2), "date", split_axis=0, concat_axis=1, tiled=True)
     g = lax.all_to_all(grad_out.transpose(1, 0, 2), "date", split_axis=0, concat_axis=1, tiled=True)
-    vd = valid_dates.T.reshape(tokens // ROWS, 1, ROWS)
     vmem = pl.BlockSpec(memory_space=pltpu.VMEM)
     gi, wg = pl.pallas_call(
         compute_kernel,
@@ -145,7 +155,7 @@
             pltpu.VMEM((tokens, 3 * width), BF16),
         ],
         compiler_params=pltpu.CompilerParams(vmem_limit_bytes=50 * 2**20),
-    )(f, g, w_qkv, w_out, vd)
+    )(f, g, w_qkv, w_out, valid_dates)
     weight_grad = lax.psum_scatter(wg, ("space", "date"), scatter_dimension=0, tiled=True)
     grad_in = lax.all_to_all(gi, "date", split_axis=1, concat_axis=0, tiled=True)
     return (grad_in.transpose(1, 0, 2), weight_grad.astype(F32))
@@ -341,7 +351,6 @@
     spaces = lax.axis_size("space")
     chunks = 4 * width // TILE
     rows = width // (4 * spaces)
-    vd = valid_dates.T.reshape(groups, 1, ROWS)
     vmem = pl.BlockSpec(memory_space=pltpu.VMEM)
     anywhere = pl.BlockSpec(memory_space=pl.ANY)
     dma = pltpu.SemaphoreType.DMA
@@ -385,7 +394,7 @@
         compiler_params=pltpu.CompilerParams(
             collective_id=0, has_side_effects=True, vmem_limit_bytes=56 * 2**20
         ),
-    )(features.transpose(1, 0, 2), grad_out.transpose(1, 0, 2), w_qkv, w_out, vd)
+    )(features.transpose(1, 0, 2), grad_out.transpose(1, 0, 2), w_qkv, w_out, valid_dates)
     return (gi.transpose(1, 0, 2), wg)
 
 

time: 78.9 us -> 76.6 us (0.971)
  Pallas kernels: 69.1 us -> 66.8 us
    pallas_call x1, Pallas kernels: 69.1 us -> 66.8 us  [local_full(): pl.pallas_call(full_kernel, out_shape=(jax.ShapeDtypeStruct((wide, near,...]
    unnamed x2 -> x3, local copies, waits for them, and re-layouts: 4.16 us -> 5.55 us
    reshape x1 -> x0, local copies, waits for them, and re-layouts: 1.34 us -> none  [local_full(): vd = valid_dates.T.reshape(groups, 1, ROWS)]
where the time goes in v3:
time: 76.6 us; the launch traced here: 76.3 us
  Pallas kernels  66.8 us (87%)
  local copies, waits for them, and re-layouts  8.92 us (12%)
    pallas_call x1, Pallas kernels, local_full(): pl.pallas_call(full_kernel, out_shape=(jax.ShapeDtypeStruct((wide, near,...  66.8 us
    unnamed x3, local copies, waits for them, and re-layouts  5.55 us
    transpose x1, local copies, waits for them, and re-layouts, local_full(): grad_out.transpose(1, 0, 2)  3.37 us

profile of v3, /device:TPU:0, one launch (start us, length us, event | category | flops | bytes accessed | tf_op | source)
XLA Modules:
  0.0 76.3 jit_solution(8376462491815853619)
XLA Ops:
  0.6 1.4 %copy.9.vd_ref = s32[64,8]{1,0:T(8,128)} copy(s32[64,8]{0,1:T(8,128)} %param.9) | data formatting | bytes 4096 | tf_op args[4]
  2.0 3.4 %copy_bitcast_fusion = (bf16[32,16,768]{2,1,0:T(8,128)(2,1)}, bf16[32,16,768]{2,1,0:T(8,128)(2,1)}) fusion(bf16[16,32,768]{2,1,0:T(8,128)(2,1)} %param.6, bf16[16,32,768]{2,1,0:T(8,128)(2,1)} %param.5), kind=kLoop, calls=%fused_computation | loop fusion | bytes 3145728 | tf_op jit(solution)/shard_map/transpose | solution.py:397
  5.4 66.8 %shard_map.68 = (bf16[32,16,768]{2,1,0:T(8,128)(2,1)}, f32[48,3072]{1,0:T(8,128)}) custom-call(bf16[32,16,768]{2,1,0:T(8,128)(2,1)} %get-tuple-element.9.f_in, bf16[32,16,768]{2,1,0:T(8,128)(2,1)} %get-tuple-element.8.g_in, bf16[768,2304]{1,0:T(8,128)(2,1)} %wq_in.1, bf16[768,768]{1,0:T(8,128)(2,1)} %wo_in.1, s32[64,8]{1,0:T(8,128)} %copy.9.vd_ref), custom_call_target="tpu_custom_call" | custom-call | tf_op jit(solution)/shard_map/pallas_call | solution.py:357
  72.1 2.2 %copy.10 = bf16[16,32,768]{2,1,0:T(8,128)(2,1)} copy(bf16[16,32,768]{2,0,1:T(8,128)(2,1)} %bitcast.5) | data formatting | bytes 1572864
  74.4 1.9 %copy.14 = f32[48,3072]{1,0:T(8,128)} copy(f32[48,3072]{1,0:T(8,128)} %get-tuple-element.13) | data formatting | bytes 1179648

commit v4 on v3

--- a/solution.py
+++ b/solution.py
@@ -43,18 +43,18 @@
     scale = 1.0 / HD**0.5
     at = pl.ds(pl.multiple_of(i * ROWS, ROWS), ROWS)
     n = ROWS // dates
-    patch = lax.broadcasted_iota(jnp.int32, vd_ref.shape, 1)
-    valid = vd_ref[...]
+    valid = vd_ref[...].astype(F32).T
+    patch = lax.broadcasted_iota(jnp.int32, valid.shape, 1)
     valid = jnp.concatenate(
         [
-            jnp.sum(jnp.where(patch == i * n + p, valid, 0), axis=1, keepdims=True)
+            jnp.sum(jnp.where(patch == i * n + p, valid, 0.0), axis=1, keepdims=True)
             for p in range(n)
         ],
         axis=0,
     )
     row = lax.broadcasted_iota(jnp.int32, (ROWS, ROWS), 0)
     col = lax.broadcasted_iota(jnp.int32, (ROWS, ROWS), 1)
-    keep = ((row // dates) == (col // dates)) & ((valid == 1) | (row == col))
+    keep = ((row // dates) == (col // dates)) & ((valid == 1.0) | (row == col))
     bias = jnp.where(keep, 0.0, -1e30).astype(F32)
     bias = jnp.concatenate([bias, bias], axis=1)
     lane = lax.broadcasted_iota(jnp.int32, (1, 2 * HD), 1)
@@ -155,7 +155,7 @@
             pltpu.VMEM((tokens, 3 * width), BF16),
         ],
         compiler_params=pltpu.CompilerParams(vmem_limit_bytes=50 * 2**20),
-    )(f, g, w_qkv, w_out, valid_dates)
+    )(f, g, w_qkv, w_out, valid_dates.T)
     weight_grad = lax.psum_scatter(wg, ("space", "date"), scatter_dimension=0, tiled=True)
     grad_in = lax.all_to_all(gi, "date", split_axis=1, concat_axis=0, tiled=True)
     return (grad_in.transpose(1, 0, 2), weight_grad.astype(F32))
@@ -163,12 +163,13 @@
 
 TILE = 256
 LAG = 2
+EARLY = 2
 MESH = pl.DeviceIdType.MESH
 
 
 def full_kernel(
     f_in, g_in, wq_in, wo_in, vd_ref, gi_out, wg_out,
-    f_ref, g_ref, wq_ref, wo_ref, nbt, qkv, da, att, dqkv, gi, part, core_in, core_sum, x_in, x_sum, z_in,
+    f_ref, g_ref, wq_ref, wo_ref, nbt, qkv, da, att, dqkv, gi, part, core_in, core_sum, x_in, x_sum, z_in, early_in, early_sum, last_in,
     load_sem, fs, fr, gs, gr, cs, cr, xs, xr, zs, zr,
 ):
     patches, dates, width = f_ref.shape
@@ -257,6 +258,26 @@
             device_id_type=MESH,
         )
 
+    def early_space(j, k):
+        return pltpu.make_async_remote_copy(
+            src_ref=core_sum.at[j, spaced(k)],
+            dst_ref=early_in.at[j, k - 1],
+            send_sem=zs.at[j, k - 1],
+            recv_sem=zr.at[j, k - 1],
+            device_id={"space": spaced(k)},
+            device_id_type=MESH,
+        )
+
+    def late_chip(j):
+        return pltpu.make_async_remote_copy(
+            src_ref=early_sum.at[j, 1 - chip],
+            dst_ref=last_in.at[j],
+            send_sem=xs.at[j],
+            recv_sem=xr.at[j],
+            device_id={"date": peers[1]},
+            device_id_type=MESH,
+        )
+
     @pl.loop(0, groups)
     def _(i):
         for r in (1, 2, 0):
@@ -299,7 +320,15 @@
             over_core(b).wait_recv()
             total = part[b, :, :, core].astype(F32) + core_in[b].astype(F32)
             core_sum[b] = total.astype(BF16)
-            over_chip(b).start()
+
+            @pl.when(b < EARLY)
+            def _():
+                for k in range(1, spaces):
+                    early_space(b, k).start()
+
+            @pl.when(b >= EARLY)
+            def _():
+                over_chip(b).start()
 
     share = chunks // groups
 
@@ -309,18 +338,31 @@
         for r in (1, 2, 0):
             backward(i, r).start()
 
+        @pl.when(i == 1)
+        def _():
+            @pl.loop(0, EARLY)
+            def _(j):
+                total = core_sum[j, space].astype(F32)
+                for k in range(1, spaces):
+                    early_space(j, k).wait_recv()
+                    total += early_in[j, k - 1].astype(F32)
+                early_sum[j] = total.astype(BF16)
+                late_chip(j).start()
+
         @pl.loop(i * share, (i + 1) * share)
         def _(j):
-            over_chip(j).wait_recv()
-            total = core_sum[j, :, chip].astype(F32) + x_in[j].astype(F32)
-            x_sum[j] = total.astype(BF16)
-            for k in range(1, spaces):
-                over_space(j, k).start()
+            @pl.when(j >= EARLY)
+            def _():
+                over_chip(j).wait_recv()
+                total = core_sum[j, :, chip].astype(F32) + x_in[j].astype(F32)
+                x_sum[j] = total.astype(BF16)
+                for k in range(1, spaces):
+                    over_space(j, k).start()
 
     own = pltpu.make_async_copy(gi.at[:, here], gi_out.at[mine], load_sem.at[0])
     own.start()
 
-    @pl.loop(0, chunks)
+    @pl.loop(EARLY, chunks)
     def _(j):
         total = x_sum[j, space].astype(F32)
         for k in range(1, spaces):
@@ -331,6 +373,16 @@
         over_chip(j).wait_send()
         for k in range(1, spaces):
             over_space(j, k).wait_send()
+
+    @pl.loop(0, EARLY)
+    def _(j):
+        late_chip(j).wait_recv()
+        total = early_sum[j, chip].astype(F32) + last_in[j].astype(F32)
+        wg_out[:, pl.ds(pl.multiple_of(j * TILE, TILE), TILE)] = total
+        over_core(j).wait_send()
+        late_chip(j).wait_send()
+        for k in range(1, spaces):
+            early_space(j, k).wait_send()
 
     own.wait()
 
@@ -379,6 +431,9 @@
             pltpu.VMEM((chunks, spaces, rows, TILE), BF16),
             pltpu.VMEM((chunks, spaces, rows, TILE), BF16),
             pltpu.VMEM((chunks, spaces - 1, rows, TILE), BF16),
+            pltpu.VMEM((EARLY, spaces - 1, 2, rows, TILE), BF16),
+            pltpu.VMEM((EARLY, 2, rows, TILE), BF16),
+            pltpu.VMEM((EARLY, rows, TILE), BF16),
             dma((4,)),
             dma((groups, 3, 2)),
             dma((groups, 3, 2)),
@@ -394,7 +449,7 @@
         compiler_params=pltpu.CompilerParams(
             collective_id=0, has_side_effects=True, vmem_limit_bytes=56 * 2**20
         ),
-    )(features.transpose(1, 0, 2), grad_out.transpose(1, 0, 2), w_qkv, w_out, valid_dates)
+    )(features.transpose(1, 0, 2), grad_out.transpose(1, 0, 2), w_qkv, w_out, valid_dates.T)
     return (gi.transpose(1, 0, 2), wg)
 
 
@@ -407,6 +462,8 @@
         and width % (16 * parts) == 0
         and features.shape[0] % 16 == 0
         and (4 * width // TILE) % (tokens // ROWS) == 0
+        and 4 * width // TILE >= EARLY * (tokens // ROWS)
+        and tokens >= 2 * ROWS
     )
     way = local_full if fits else local_plain
     return way(features, grad_out, w_qkv, w_out, valid_dates)

time: 76.6 us -> 72.8 us (0.950)
  Pallas kernels: 66.8 us -> 64.4 us
  local copies, waits for them, and re-layouts: 8.92 us -> 7.53 us
    pallas_call x1, Pallas kernels: 66.8 us -> 64.4 us  [local_full(): pl.pallas_call(full_kernel, out_shape=(jax.ShapeDtypeStruct((wide, near,...]
    unnamed x3 -> x2, local copies, waits for them, and re-layouts: 5.55 us -> 4.16 us
where the time goes in v4:
time: 72.8 us; the launch traced here: 72.6 us
  Pallas kernels  64.4 us (88%)
  local copies, waits for them, and re-layouts  7.53 us (10%)
    pallas_call x1, Pallas kernels, local_full(): pl.pallas_call(full_kernel, out_shape=(jax.ShapeDtypeStruct((wide, near,...  64.4 us
    unnamed x2, local copies, waits for them, and re-layouts  4.16 us
    transpose x1, local copies, waits for them, and re-layouts, local_full(): grad_out.transpose(1, 0, 2)  3.37 us

profile of v4, /device:TPU:0, one launch (start us, length us, event | category | flops | bytes accessed | tf_op | source)
XLA Modules:
  0.0 72.6 jit_solution(13355994482255983734)
XLA Ops:
  0.6 3.4 %copy_bitcast_fusion = (bf16[32,16,768]{2,1,0:T(8,128)(2,1)}, bf16[32,16,768]{2,1,0:T(8,128)(2,1)}) fusion(bf16[16,32,768]{2,1,0:T(8,128)(2,1)} %param.6, bf16[16,32,768]{2,1,0:T(8,128)(2,1)} %param.5), kind=kLoop, calls=%fused_computation | loop fusion | bytes 3145728 | tf_op jit(solution)/shard_map/transpose | solution.py:452
  4.0 64.4 %shard_map.68 = (bf16[32,16,768]{2,1,0:T(8,128)(2,1)}, f32[48,3072]{1,0:T(8,128)}) custom-call(bf16[32,16,768]{2,1,0:T(8,128)(2,1)} %get-tuple-element.9.f_in, bf16[32,16,768]{2,1,0:T(8,128)(2,1)} %get-tuple-element.8.g_in, bf16[768,2304]{1,0:T(8,128)(2,1)} %wq_in.1, bf16[768,768]{1,0:T(8,128)(2,1)} %wo_in.1, s32[8,64]{1,0:T(8,128)} %bitcast.7), custom_call_target="tpu_custom_call" | custom-call | tf_op jit(solution)/shard_map/pallas_call | solution.py:409
  68.4 2.2 %copy.9 = bf16[16,32,768]{2,1,0:T(8,128)(2,1)} copy(bf16[16,32,768]{2,0,1:T(8,128)(2,1)} %bitcast.6) | data formatting | bytes 1572864
  70.6 1.9 %copy.13 = f32[48,3072]{1,0:T(8,128)} copy(f32[48,3072]{1,0:T(8,128)} %get-tuple-element.13) | data formatting | bytes 1179648

commit v5 on v4

--- a/solution.py
+++ b/solution.py
@@ -163,7 +163,7 @@
 
 TILE = 256
 LAG = 2
-EARLY = 2
+EARLY = 1
 MESH = pl.DeviceIdType.MESH
 
 
@@ -287,8 +287,17 @@
     for copy in loads:
         copy.wait()
 
+    def give_back(i):
+        gi[pl.ds(i * n, n)] = norm_backward(i, f_ref, g_ref, wq_ref, dqkv).reshape(n, dates, width)
+        for r in (1, 2, 0):
+            backward(i, r).start()
+
     @pl.loop(0, groups)
     def _(i):
+        @pl.when(i > 0)
+        def _():
+            give_back(i - 1)
+
         for r in range(3):
             for a in range(2):
                 forward(i, r, a).wait_recv()
@@ -334,9 +343,9 @@
 
     @pl.loop(0, groups)
     def _(i):
-        gi[pl.ds(i * n, n)] = norm_backward(i, f_ref, g_ref, wq_ref, dqkv).reshape(n, dates, width)
-        for r in (1, 2, 0):
-            backward(i, r).start()
+        @pl.when(i == 0)
+        def _():
+            give_back(groups - 1)
 
         @pl.when(i == 1)
         def _():

time: 72.8 us -> 74.1 us (1.018)
  Pallas kernels: 64.4 us -> 65.7 us
    pallas_call x1, Pallas kernels: 64.4 us -> 65.7 us  [local_full(): pl.pallas_call(full_kernel, out_shape=(jax.ShapeDtypeStruct((wide, near,...]
where the time goes in v5:
time: 74.1 us; the launch traced here: 73.9 us
  Pallas kernels  65.7 us (89%)
  local copies, waits for them, and re-layouts  7.53 us (10%)
    pallas_call x1, Pallas kernels, local_full(): pl.pallas_call(full_kernel, out_shape=(jax.ShapeDtypeStruct((wide, near,...  65.7 us
    unnamed x2, local copies, waits for them, and re-layouts  4.16 us
    transpose x1, local copies, waits for them, and re-layouts, local_full(): grad_out.transpose(1, 0, 2)  3.37 us

profile of v5, /device:TPU:0, one launch (start us, length us, event | category | flops | bytes accessed | tf_op | source)
XLA Modules:
  0.0 73.9 jit_solution(10216562919332339947)
XLA Ops:
  0.6 3.4 %copy_bitcast_fusion = (bf16[32,16,768]{2,1,0:T(8,128)(2,1)}, bf16[32,16,768]{2,1,0:T(8,128)(2,1)}) fusion(bf16[16,32,768]{2,1,0:T(8,128)(2,1)} %param.6, bf16[16,32,768]{2,1,0:T(8,128)(2,1)} %param.5), kind=kLoop, calls=%fused_computation | loop fusion | bytes 3145728 | tf_op jit(solution)/shard_map/transpose | solution.py:461
  4.0 65.7 %shard_map.68 = (bf16[32,16,768]{2,1,0:T(8,128)(2,1)}, f32[48,3072]{1,0:T(8,128)}) custom-call(bf16[32,16,768]{2,1,0:T(8,128)(2,1)} %get-tuple-element.9.f_in, bf16[32,16,768]{2,1,0:T(8,128)(2,1)} %get-tuple-element.8.g_in, bf16[768,2304]{1,0:T(8,128)(2,1)} %wq_in.1, bf16[768,768]{1,0:T(8,128)(2,1)} %wo_in.1, s32[8,64]{1,0:T(8,128)} %bitcast.7), custom_call_target="tpu_custom_call" | custom-call | tf_op jit(solution)/shard_map/pallas_call | solution.py:418
  69.7 2.2 %copy.9 = bf16[16,32,768]{2,1,0:T(8,128)(2,1)} copy(bf16[16,32,768]{2,0,1:T(8,128)(2,1)} %bitcast.6) | data formatting | bytes 1572864
  71.9 1.9 %copy.13 = f32[48,3072]{1,0:T(8,128)} copy(f32[48,3072]{1,0:T(8,128)} %get-tuple-element.13) | data formatting | bytes 1179648

commit v6 on v4

--- a/solution.py
+++ b/solution.py
@@ -163,7 +163,7 @@
 
 TILE = 256
 LAG = 2
-EARLY = 2
+EARLY = 3
 MESH = pl.DeviceIdType.MESH
 
 
@@ -338,7 +338,7 @@
         for r in (1, 2, 0):
             backward(i, r).start()
 
-        @pl.when(i == 1)
+        @pl.when(i == 2)
         def _():
             @pl.loop(0, EARLY)
             def _(j):
@@ -463,7 +463,7 @@
         and features.shape[0] % 16 == 0
         and (4 * width // TILE) % (tokens // ROWS) == 0
         and 4 * width // TILE >= EARLY * (tokens // ROWS)
-        and tokens >= 2 * ROWS
+        and tokens >= 3 * ROWS
     )
     way = local_full if fits else local_plain
     return way(features, grad_out, w_qkv, w_out, valid_dates)

time: 72.8 us -> 73.3 us (level)
  no operation moved by 1% of the time
where the time goes in v6:
time: 73.3 us; the launch traced here: 73 us
  Pallas kernels  64.8 us (88%)
  local copies, waits for them, and re-layouts  7.53 us (10%)
    pallas_call x1, Pallas kernels, local_full(): pl.pallas_call(full_kernel, out_shape=(jax.ShapeDtypeStruct((wide, near,...  64.8 us
    unnamed x2, local copies, waits for them, and re-layouts  4.16 us
    transpose x1, local copies, waits for them, and re-layouts, local_full(): grad_out.transpose(1, 0, 2)  3.37 us

profile of v6, /device:TPU:0, one launch (start us, length us, event | category | flops | bytes accessed | tf_op | source)
XLA Modules:
  0.0 73.0 jit_solution(10686186602623985141)
XLA Ops:
  0.6 3.4 %copy_bitcast_fusion = (bf16[32,16,768]{2,1,0:T(8,128)(2,1)}, bf16[32,16,768]{2,1,0:T(8,128)(2,1)}) fusion(bf16[16,32,768]{2,1,0:T(8,128)(2,1)} %param.6, bf16[16,32,768]{2,1,0:T(8,128)(2,1)} %param.5), kind=kLoop, calls=%fused_computation | loop fusion | bytes 3145728 | tf_op jit(solution)/shard_map/transpose | solution.py:452
  4.0 64.8 %shard_map.68 = (bf16[32,16,768]{2,1,0:T(8,128)(2,1)}, f32[48,3072]{1,0:T(8,128)}) custom-call(bf16[32,16,768]{2,1,0:T(8,128)(2,1)} %get-tuple-element.9.f_in, bf16[32,16,768]{2,1,0:T(8,128)(2,1)} %get-tuple-element.8.g_in, bf16[768,2304]{1,0:T(8,128)(2,1)} %wq_in.1, bf16[768,768]{1,0:T(8,128)(2,1)} %wo_in.1, s32[8,64]{1,0:T(8,128)} %bitcast.7), custom_call_target="tpu_custom_call" | custom-call | tf_op jit(solution)/shard_map/pallas_call | solution.py:409
  68.8 2.2 %copy.9 = bf16[16,32,768]{2,1,0:T(8,128)(2,1)} copy(bf16[16,32,768]{2,0,1:T(8,128)(2,1)} %bitcast.6) | data formatting | bytes 1572864
  71.1 1.9 %copy.13 = f32[48,3072]{1,0:T(8,128)} copy(f32[48,3072]{1,0:T(8,128)} %get-tuple-element.13) | data formatting | bytes 1179648
